TPU v7x, 32 devices: a whole 2x2x4 slice. The times are simulated.
32 devices in a mesh: grp: 2 (over x), seq: 8 (over z, y), row: 2 (over core).
Axes of the slice: x: 2, y: 2, z: 4, core: 2. Of those that a mesh axis runs over, the one named last changes fastest.
Arguments:
- left_act: bfloat16 [128, 256, 32], P(('grp', 'seq'), 'row'), parts along dimension 0, may hold values from -6 to 6
- right_act: bfloat16 [128, 384, 32], P(('grp', 'seq')), parts along dimension 0, may hold values from -6 to 6
- pair_grad: bfloat16 [512, 384, 128], P(('grp', 'row'), 'seq'), parts along dimension 0, may hold values from -24 to 24
- out_weight: bfloat16 [1024, 128], replicated, may hold values from -0.1875 to 0.1875
- seq_mask: int32 [128], P(('grp', 'seq')), parts along dimension 0, may hold values from 0 to 1, as said below
Outputs:
- grad_left: bfloat16 [128, 256, 32], P(('grp', 'seq'), 'row'), parts along dimension 0
- grad_right: bfloat16 [128, 384, 32], P(('grp', 'seq'), 'row'), parts along dimension 0
- grad_weight: float32 [2048, 128], P('grp'), parts along dimension 0
There are 2 independent parts, one for each index of `grp`. A program takes and returns all parts, laid end to end along the dimension named above; an argument that names none is the same for every part. Nothing has to cross between parts.
Inputs may be any that keep to these rules, and one draw needn't show every extreme that they name: `seq_mask`: entry 0 (the query sequence) is 1.
All inputs are finite; a program needn't handle non-finite values.
Results may differ from a plain program's by a relative error of at most 0.001.
Values may be sent and summed in bfloat16 or wider, within the bound.
A program may use at most 128 MiB of HBM per device.

v0:
```python
import functools

import jax
import jax.numpy as jnp
from jax import lax
from jax.experimental import pallas as pl
from jax.experimental.pallas import tpu as pltpu
from jax.sharding import PartitionSpec as P

NT = (((1,), (1,)), ((), ()))
NN = (((1,), (0,)), ((), ()))
MESH = pl.DeviceIdType.MESH
GL_LANES = 1024
LANE = 128


def block_cols(cols):
    return max(n for n in (2, 4, 6, 8) if cols % n == 0)


def dot(lhs, rhs, dims):
    return lax.dot_general(lhs, rhs, dims, preferred_element_type=jnp.float32)


def split(value):
    high = value.astype(jnp.bfloat16)
    low = (value - high.astype(jnp.float32)).astype(jnp.bfloat16)
    return high, low


def kernel(
    shards, chans, p_ref, w_ref, l_in, r_in, gl_out, gr_out, gw_out,
    qh, ql, oh, ol, l_all, r_all, left, right, right_t,
    part, gly, gls, glz, gr_t, gr_r, gr_b, gr_in,
    gw_acc, gw_r, gw_s1, gw_y, gw_s2, gw_z, gw_f,
    r_sem, lz_sem, ly_sem, gly_sem, glz_sem, grr_sem, gr_sem, gws_sem, gwz_sem, gwg_sem,
):
    cols, rows, width = p_ref.shape
    nz = shards // 2
    chunks = part.shape[0]
    seq_rows = l_in.shape[0]
    seqs = shards * seq_rows
    step_cols = block_cols(cols)
    steps = cols // step_cols
    jb = step_cols * chans
    own_cols = cols * chans
    me = lax.axis_index("seq")
    row = lax.axis_index("row")
    y, z = lax.rem(me, 2), lax.div(me, 2)
    ypeer, zs = z * 2 + 1 - y, [lax.rem(z + d, nz) for d in range(nz)]
    sent = []

    def send(src, dst, sems, at, where, recv_at=None):
        copy = pltpu.make_async_remote_copy(
            src_ref=src, dst_ref=dst, send_sem=sems.at[(0,) + at],
            recv_sem=sems.at[(1,) + (at if recv_at is None else recv_at)],
            device_id=where, device_id_type=MESH,
        )
        copy.start()
        return copy

    def arrive(dst, sems, at):
        pltpu.make_async_remote_copy(
            src_ref=dst, dst_ref=dst, send_sem=sems.at[(0,) + at], recv_sem=sems.at[(1,) + at],
            device_id={"seq": ypeer}, device_id_type=MESH,
        ).wait_recv()

    barrier = pltpu.get_barrier_semaphore()
    for o in range(1, shards):
        pl.semaphore_signal(barrier, inc=1, device_id={"seq": lax.rem(me + o, shards)}, device_id_type=MESH)
    pl.semaphore_signal(barrier, inc=1, device_id={"row": 1 - row}, device_id_type=MESH)
    pl.semaphore_wait(barrier, shards)

    for o in range(1, shards):
        e = lax.rem(me + o, shards)
        sent.append(send(r_in.at[e], r_all.at[me], r_sem, (o,), {"seq": e}))
    for d in range(1, nz):
        sent.append(send(l_in, l_all.at[me], lz_sem, (d,), {"seq": zs[d] * 2 + y}))
    sent.append(send(l_in, l_all.at[me], ly_sem, (0,), {"seq": ypeer}))
    l_all[me] = l_in[...]
    r_all[me] = r_in[me]

    def project(jp, carry):
        block = p_ref[pl.ds(jp * 2, 2)].reshape(2 * rows, width)
        for ac in range(0, chans, 4):
            q = dot(w_ref[ac * chans : (ac + 4) * chans, :], block, NT)
            high, low = split(q)
            for a in range(4):
                for jj in range(2):
                    base = pl.multiple_of((jp * 2 + jj) * chans, chans)
                    to = (pl.ds(base, chans), slice((ac + a) * rows, (ac + a + 1) * rows))
                    at = (slice(a * chans, (a + 1) * chans), slice(jj * rows, (jj + 1) * rows))
                    qh[to] = high[at]
                    ql[to] = low[at]
        return carry

    pairs = cols // 2
    lax.fori_loop(0, pairs // 2, project, 0)
    for d in range(1, nz):
        src = lax.rem(z + nz - d, nz) * 2 + y
        arrive(l_all.at[src], lz_sem, (d,))
        sent.append(send(l_all.at[src], l_all.at[src], ly_sem, (d,), {"seq": ypeer}))
    lax.fori_loop(pairs // 2, pairs, project, 0)

    for o in range(1, shards):
        arrive(r_all.at[lax.rem(me + shards - o, shards)], r_sem, (o,))
    rfull = r_all[...].astype(jnp.float32).reshape(seqs, LANE + own_cols)
    mask_all = rfull[:, :LANE]
    count = jnp.sum(mask_all, axis=0, keepdims=True)
    scale_all = mask_all / count
    scale_mine = r_in[me].astype(jnp.float32)[:, :LANE] / count
    right[...] = rfull[:, LANE:].astype(jnp.bfloat16)
    right_t[...] = rfull[:, LANE:].T.astype(jnp.bfloat16)

    for c in range(chunks):
        for t in range(0, GL_LANES, 256):
            at = slice(c * GL_LANES + t, c * GL_LANES + t + 256)
            g = dot(right[...], qh[:, at], NN) + dot(right[...], ql[:, at], NN)
            g = g.reshape(nz, 2, seq_rows, 256)
            for half in range(2):
                part[c, half, :, :, t : t + 256] = g[:, half]
        sent.append(send(part.at[c, 1 - y], gly.at[c], gly_sem, (c,), {"seq": ypeer}))

    for d in range(nz):
        src = lax.rem(z + nz - d, nz) * 2 + 1 - y
        arrive(l_all.at[src], ly_sem, (d,))
    left[...] = l_all[...].astype(jnp.float32).reshape(seqs, -1).astype(jnp.bfloat16)

    def gl_second(c):
        arrive(gly.at[c], gly_sem, (c,))
        gls[c] = part[c, y] + gly[c]
        for d in range(1, nz):
            sent.append(send(gls.at[c, zs[d]], glz.at[c, z], glz_sem, (c, d), {"seq": zs[d] * 2 + y}))

    def gl_last(c):
        total = gls[c, z]
        for d in range(1, nz):
            src = lax.rem(z + nz - d, nz)
            arrive(glz.at[c, src], glz_sem, (c, d))
            total += glz[c, src]
        gl_out[:, c * GL_LANES : (c + 1) * GL_LANES] = (total * scale_mine[:, :1]).astype(jnp.bfloat16)

    gw_acc[...] = jnp.zeros_like(gw_acc)

    def weight_step(step, carry):
        rt = right_t[pl.ds(pl.multiple_of(step * jb, jb), jb), :]
        for ac in range(0, chans, 2):
            at = slice(ac * rows, (ac + 2) * rows)
            oh[:, at], ol[:, at] = split(dot(rt, left[:, at], NN))
        for ac in range(0, chans, 8):
            total = gw_acc[ac * chans : (ac + 8) * chans, :]
            for jp in range(step_cols // 2):
                block = p_ref[pl.ds(step * step_cols + 2 * jp, 2)].reshape(2 * rows, width)
                for src in (oh, ol):
                    lhs = jnp.concatenate(
                        [
                            jnp.concatenate(
                                [
                                    src[j * chans : (j + 1) * chans, a * rows : (a + 1) * rows]
                                    for j in (2 * jp, 2 * jp + 1)
                                ],
                                axis=1,
                            )
                            for a in range(ac, ac + 8)
                        ],
                        axis=0,
                    )
                    total += dot(lhs, block, NN)
            gw_acc[ac * chans : (ac + 8) * chans, :] = total
        return carry

    lax.fori_loop(0, steps // 2, weight_step, 0)
    for c in range(chunks // 2):
        gl_second(c)
    lax.fori_loop(steps // 2, steps, weight_step, 0)

    half_rows, quarter, last = gw_r.shape[0], gw_y.shape[0], gw_z.shape[1]

    def span(start, size):
        return pl.ds(pl.multiple_of(start, 8), size)

    def gw_row():
        sent.append(send(gw_acc.at[span((1 - row) * half_rows, half_rows)], gw_r, gws_sem, (0,), {"row": 1 - row}))

    def gw_ypair():
        arrive(gw_r, gws_sem, (0,))
        gw_s1[...] = gw_acc[span(row * half_rows, half_rows), :] + gw_r[...]
        sent.append(send(gw_s1.at[span((1 - y) * quarter, quarter)], gw_y, gws_sem, (1,), {"seq": ypeer}))

    def gw_zs():
        arrive(gw_y, gws_sem, (1,))
        gw_s2[...] = gw_s1[span(y * quarter, quarter), :] + gw_y[...]
        for d in range(1, nz):
            sent.append(send(gw_s2.at[span(zs[d] * last, last)], gw_z.at[z], gwz_sem, (d,), {"seq": zs[d] * 2 + y}))

    def gw_place(r, yy, zz):
        return r * half_rows + yy * quarter + zz * last

    def gw_final():
        total = gw_s2[span(z * last, last), :]
        for d in range(1, nz):
            src = lax.rem(z + nz - d, nz)
            arrive(gw_z.at[src], gwz_sem, (d,))
            total += gw_z[src]
        mine = span(gw_place(row, y, z), last)
        gw_f[mine, :] = total / count
        for d in range(1, nz):
            sent.append(send(gw_f.at[mine], gw_f.at[mine], gwg_sem, (d,), {"seq": zs[d] * 2 + y}))

    def gw_gather_y():
        for d in range(1, nz):
            arrive(gw_f.at[span(gw_place(row, y, lax.rem(z + nz - d, nz)), last)], gwg_sem, (d,))
        mine = span(gw_place(row, y, 0), quarter)
        sent.append(send(gw_f.at[mine], gw_f.at[mine], gws_sem, (2,), {"seq": ypeer}))

    def gw_gather_row():
        arrive(gw_f.at[span(gw_place(row, 1 - y, 0), quarter)], gws_sem, (2,))
        mine = span(gw_place(row, 0, 0), half_rows)
        sent.append(send(gw_f.at[mine], gw_f.at[mine], gws_sem, (3,), {"row": 1 - row}))

    def gw_done():
        arrive(gw_f.at[span(gw_place(1 - row, 0, 0), half_rows)], gws_sem, (3,))
        gw_out[...] = gw_f[...]

    gw_row()
    for c in range(chunks // 2, chunks):
        gl_second(c)

    between = {0: gw_ypair, 1: gw_zs, 3: gw_final, 4: gw_gather_y}
    for step in range(max(steps, 6)):
        if step < steps:
            at = slice(step * jb, (step + 1) * jb)
            g = dot(qh[at, :], left[...], NT) + dot(ql[at, :], left[...], NT)
            gr_t[:, :, at] = g.T.reshape(shards, seq_rows, jb)
        if step in between:
            between[step]()

    collector = lax.div(me, nz) == row
    slot = lax.rem(me, nz)

    def row_copy():
        return pltpu.make_async_remote_copy(
            src_ref=gr_t, dst_ref=gr_r, send_sem=grr_sem.at[0], recv_sem=grr_sem.at[1],
            device_id={"row": 1 - row}, device_id_type=MESH,
        )

    def right_copy(o):
        e = lax.rem(me + o, shards)
        return pltpu.make_async_remote_copy(
            src_ref=gr_b.at[e], dst_ref=gr_in.at[slot], send_sem=gr_sem.at[0, o], recv_sem=gr_sem.at[1, slot],
            device_id={"seq": e}, device_id_type=MESH,
        )

    @pl.when(jnp.logical_not(collector))
    def _():
        row_copy().start()

    gw_gather_row()

    @pl.when(collector)
    def _():
        row_copy().wait_recv()
        scale3 = scale_all.reshape(shards, seq_rows, LANE)[:, :, :1]
        gr_b[...] = ((gr_t[...] + gr_r[...]) * scale3).astype(jnp.bfloat16)
        for o in range(1, shards):
            right_copy(o).start()
        gr_in[slot] = gr_b[me]

    for c in range(chunks):
        gl_last(c)
    gw_done()

    for k in range(nz):
        @pl.when(row * nz + k != me)
        def _():
            arrive(gr_in.at[k], gr_sem, (k,))

    gr_out[...] = gr_in[...]

    @pl.when(collector)
    def _():
        for o in range(1, shards):
            right_copy(o).wait_send()

    @pl.when(jnp.logical_not(collector))
    def _():
        row_copy().wait_send()

    for copy in sent:
        copy.wait_send()


def all_grads(pair_t, weight, left, right, chans):
    cols, rows, width = pair_t.shape
    shards, seq_rows, _ = right.shape
    nz = shards // 2
    seqs = shards * seq_rows
    lanes = chans * rows
    own = cols * chans
    jb = block_cols(cols) * chans
    chunks = lanes // GL_LANES
    total = chans * chans
    half, quarter, last = total // 2, total // 4, total // 4 // nz
    f32, bf16 = jnp.float32, jnp.bfloat16
    flops = 2 * cols * rows * chans * chans * (width * 3 + seqs * 5)
    vmem = pl.BlockSpec(memory_space=pltpu.VMEM)
    sem = pltpu.SemaphoreType.DMA
    return pl.pallas_call(
        functools.partial(kernel, shards, chans),
        in_specs=[vmem] * 4,
        out_specs=[vmem] * 3,
        out_shape=[
            jax.ShapeDtypeStruct((seq_rows, lanes), bf16),
            jax.ShapeDtypeStruct((nz, seq_rows, own), bf16),
            jax.ShapeDtypeStruct((total, width), f32),
        ],
        scratch_shapes=[
            pltpu.VMEM((own, lanes), bf16),
            pltpu.VMEM((own, lanes), bf16),
            pltpu.VMEM((jb, lanes), bf16),
            pltpu.VMEM((jb, lanes), bf16),
            pltpu.VMEM((shards, seq_rows, lanes), bf16),
            pltpu.VMEM((shards, seq_rows, LANE + own), bf16),
            pltpu.VMEM((seqs, lanes), bf16),
            pltpu.VMEM((seqs, own), bf16),
            pltpu.VMEM((own, seqs), bf16),
            pltpu.VMEM((chunks, 2, nz, seq_rows, GL_LANES), f32),
            pltpu.VMEM((chunks, nz, seq_rows, GL_LANES), f32),
            pltpu.VMEM((chunks, nz, seq_rows, GL_LANES), f32),
            pltpu.VMEM((chunks, nz, seq_rows, GL_LANES), f32),
            pltpu.VMEM((shards, seq_rows, own), f32),
            pltpu.VMEM((shards, seq_rows, own), f32),
            pltpu.VMEM((shards, seq_rows, own), bf16),
            pltpu.VMEM((nz, seq_rows, own), bf16),
            pltpu.VMEM((total, width), f32),
            pltpu.VMEM((half, width), f32),
            pltpu.VMEM((half, width), f32),
            pltpu.VMEM((quarter, width), f32),
            pltpu.VMEM((quarter, width), f32),
            pltpu.VMEM((nz, last, width), f32),
            pltpu.VMEM((total, width), f32),
            sem((2, shards)),
            sem((2, nz)),
            sem((2, nz)),
            sem((2, chunks)),
            sem((2, chunks, nz)),
            sem((2,)),
            sem((2, shards)),
            sem((2, 4)),
            sem((2, nz)),
            sem((2, nz)),
        ],
        compiler_params=pltpu.CompilerParams(
            vmem_limit_bytes=56 * 2**20, collective_id=0, has_side_effects=True
        ),
        cost_estimate=pl.CostEstimate(flops=flops, bytes_accessed=6 * 2**20, transcendentals=0),
        name="all_grads",
    )(pair_t, weight, left, right)


def body(left_act, right_act, pair_grad, out_weight, seq_mask):
    seq_rows, pair_rows, chans = left_act.shape
    shards = lax.axis_size("seq")
    cols = right_act.shape[1]
    mask_half = seq_mask.astype(jnp.bfloat16)[:, None, None]
    left = (left_act * mask_half).transpose(0, 2, 1).reshape(seq_rows, chans * pair_rows)
    right = (right_act * mask_half).reshape(seq_rows, shards, -1)
    marks = jnp.broadcast_to(mask_half, (seq_rows, shards, LANE))
    right = jnp.concatenate([marks, right], axis=2).transpose(1, 0, 2)
    gl, gr, gw = all_grads(pair_grad.transpose(1, 0, 2), out_weight, left, right, chans)
    grad_left = gl.reshape(seq_rows, chans, pair_rows).transpose(0, 2, 1)
    grad_right = gr.transpose(1, 0, 2).reshape(seq_rows, -1, chans)
    return (grad_left, grad_right, gw)


def solution(mesh):
    placed = (
        P(("grp", "seq"), "row", None),
        P(("grp", "seq"), None, None),
        P(("grp", "row"), "seq", None),
        P(),
        P(("grp", "seq")),
    )
    return jax.shard_map(
        body,
        mesh=mesh,
        in_specs=placed,
        out_specs=(P(("grp", "seq"), "row", None), P(("grp", "seq"), "row", None), P("grp", None)),
        check_vma=False,
    )
```

profile of v0, /device:TPU:1, one launch (start us, length us, event | category | flops | bytes accessed | tf_op | source)
XLA Modules:
  0.0 75.3 jit_solution(9958098419329265203)
XLA Ops:
  0.6 0.7 convert_element_type.3
  1.3 0.1 broadcast_in_dim.2
  1.4 0.9 %multiply_bitcast_fusion = bf16[1,8,32,128]{3,2,1,0:T(8,128)(2,1)S(1)} fusion(bf16[8,128,32]{1,2,0:T(8,128)(2,1)} %param.5, bf16[8]{0:T(256)(128)(2,1)S(1)} %convert_element_type.3), kind=kLoop, calls=%fused_computation.5 | loop fusion | flops 32768 | bytes 131088
  2.3 0.7 copy.21
  2.9 0.0 copy-start
  2.9 1.1 %broadcast_multiply_fusion = bf16[8,384,32]{1,2,0:T(8,128)(2,1)S(1)} fusion(bf16[8,384,32]{1,2,0:T(8,128)(2,1)} %param.6, bf16[8]{0:T(256)(128)(2,1)S(1)} %convert_element_type.3), kind=kLoop, calls=%fused_computation.2 | loop fusion | flops 98304 | bytes 393232 | tf_op jit(solution)/shard_map/mul | solution.py:367
  4.1 0.4 copy.11
  4.5 0.7 reshape.20
  5.2 0.1 copy.12
  5.3 0.7 maximum_bitcast_fusion.r_in
  6.0 0.0 copy-done
  6.0 1.6 %copy.20 = bf16[128,48,128]{2,0,1:T(8,128)(2,1)} copy(bf16[128,48,128]{2,1,0:T(8,128)(2,1)S(1)} %copy-done) | data formatting | bytes 3145728 | tf_op args[2]
  7.5 63.4 %all_grads.1 = (bf16[8,4096]{1,0:T(8,128)(2,1)}, bf16[4,8,1536]{2,1,0:T(8,128)(2,1)}, f32[1024,128]{1,0:T(8,128)}) custom-call(bf16[48,128,128]{2,1,0:T(8,128)(2,1)} %bitcast.16, bf16[1024,128]{1,0:T(8,128)(2,1)} %w_ref.1, bf16[8,4096]{1,0:T(8,128)(2,1)} %bitcast.18, bf16[8,8,1664]{2,1,0:T(8,128)(2,1)} %maximum_bitcast_fusion.r_in), custom_call_target="tpu_custom_call" | custom-call | flops 8858370048 | bytes 6291456 | tf_op jit(solution)/shard_map/all_grads/pallas_call | solution.py:308
  70.9 0.0 copy-start.1
  70.9 1.5 %copy.22 = bf16[8,32,128]{2,1,0:T(8,128)(2,1)} copy(bf16[8,32,128]{2,0,1:T(8,128)(2,1)} %bitcast.20) | data formatting | bytes 131072 | tf_op jit(solution)/shard_map/reshape | solution.py:371
  72.5 0.9 %copy.14 = bf16[8,4,1536]{2,1,0:T(4,128)(2,1)S(1)} copy(bf16[8,4,1536]{2,0,1:T(8,128)(2,1)} %bitcast.17) | data formatting | bytes 196608 | tf_op jit(solution)/shard_map/transpose | solution.py:372
  73.4 0.2 reshape.22
  73.6 0.8 %copy.15 = bf16[8,192,32]{1,2,0:T(8,128)(2,1)} copy(bf16[8,192,32]{2,1,0:T(8,128)(2,1)S(1)} %reshape.22) | data formatting | bytes 196608
  74.5 0.0 copy-done.1
  74.5 0.8 %copy.24 = f32[1024,128]{1,0:T(8,128)} copy(f32[1024,128]{1,0:T(8,128)S(1)} %copy-done.1) | data formatting | bytes 1048576
Async XLA Ops:
  2.9 3.0 %copy-start = (bf16[128,48,128]{2,1,0:T(8,128)(2,1)S(1)}, bf16[128,48,128]{2,1,0:T(8,128)(2,1)}, u32[]{:S(2)}) copy-start(bf16[128,48,128]{2,1,0:T(8,128)(2,1)} %param.7) | copy-start | bytes 4718596
  70.9 3.6 %copy-start.1 = (f32[1024,128]{1,0:T(8,128)S(1)}, f32[1024,128]{1,0:T(8,128)}, u32[]{:S(2)}) copy-start(f32[1024,128]{1,0:T(8,128)} %get-tuple-element.17) | copy-start | bytes 1572868
where the time goes:
time: 75.5 us; the launch traced here: 75.3 us
  Pallas kernels  63.4 us (84%)
  local copies, waits for them, and re-layouts  7.81 us (10%)
  other arithmetic  3.41 us (5%)
    pallas_call x1, Pallas kernels, all_grads(): pl.pallas_call(functools.partial(kernel, shards, chans), in_specs=[vmem]...  63.4 us
    unnamed x8, local copies, waits for them, and re-layouts  3.89 us
    reshape x1, local copies, waits for them, and re-layouts, body(): grad_left = gl.reshape(seq_rows, chans, pair_rows).transpose(0, 2, 1)  1.54 us

commit v1 on v0

--- a/solution.py
+++ b/solution.py
@@ -12,6 +12,8 @@
 MESH = pl.DeviceIdType.MESH
 GL_LANES = 1024
 LANE = 128
+PROJECT = 4
+HALVES = 2
 
 
 def block_cols(cols):
@@ -74,18 +76,15 @@
     for o in range(1, shards):
         e = lax.rem(me + o, shards)
         sent.append(send(r_in.at[e], r_all.at[me], r_sem, (o,), {"seq": e}))
-    for d in range(1, nz):
-        sent.append(send(l_in, l_all.at[me], lz_sem, (d,), {"seq": zs[d] * 2 + y}))
-    sent.append(send(l_in, l_all.at[me], ly_sem, (0,), {"seq": ypeer}))
     l_all[me] = l_in[...]
     r_all[me] = r_in[me]
 
     def project(jp, carry):
         block = p_ref[pl.ds(jp * 2, 2)].reshape(2 * rows, width)
-        for ac in range(0, chans, 4):
-            q = dot(w_ref[ac * chans : (ac + 4) * chans, :], block, NT)
+        for ac in range(0, chans, PROJECT):
+            q = dot(w_ref[ac * chans : (ac + PROJECT) * chans, :], block, NT)
             high, low = split(q)
-            for a in range(4):
+            for a in range(PROJECT):
                 for jj in range(2):
                     base = pl.multiple_of((jp * 2 + jj) * chans, chans)
                     to = (pl.ds(base, chans), slice((ac + a) * rows, (ac + a + 1) * rows))
@@ -95,12 +94,12 @@
         return carry
 
     pairs = cols // 2
-    lax.fori_loop(0, pairs // 2, project, 0)
+    first = pairs // 6
+    lax.fori_loop(0, first, project, 0)
     for d in range(1, nz):
-        src = lax.rem(z + nz - d, nz) * 2 + y
-        arrive(l_all.at[src], lz_sem, (d,))
-        sent.append(send(l_all.at[src], l_all.at[src], ly_sem, (d,), {"seq": ypeer}))
-    lax.fori_loop(pairs // 2, pairs, project, 0)
+        sent.append(send(l_in, l_all.at[me], lz_sem, (d,), {"seq": zs[d] * 2 + y}))
+    sent.append(send(l_in, l_all.at[me], ly_sem, (0,), {"seq": ypeer}))
+    lax.fori_loop(first, pairs, project, 0)
 
     for o in range(1, shards):
         arrive(r_all.at[lax.rem(me + shards - o, shards)], r_sem, (o,))
@@ -112,7 +111,7 @@
     right[...] = rfull[:, LANE:].astype(jnp.bfloat16)
     right_t[...] = rfull[:, LANE:].T.astype(jnp.bfloat16)
 
-    for c in range(chunks):
+    def gl_first(c):
         for t in range(0, GL_LANES, 256):
             at = slice(c * GL_LANES + t, c * GL_LANES + t + 256)
             g = dot(right[...], qh[:, at], NN) + dot(right[...], ql[:, at], NN)
@@ -121,6 +120,15 @@
                 part[c, half, :, :, t : t + 256] = g[:, half]
         sent.append(send(part.at[c, 1 - y], gly.at[c], gly_sem, (c,), {"seq": ypeer}))
 
+    early = chunks
+    gl_first(0)
+    for d in range(1, nz):
+        src = lax.rem(z + nz - d, nz) * 2 + y
+        arrive(l_all.at[src], lz_sem, (d,))
+        sent.append(send(l_all.at[src], l_all.at[src], ly_sem, (d,), {"seq": ypeer}))
+    for c in range(1, early):
+        gl_first(c)
+
     for d in range(nz):
         src = lax.rem(z + nz - d, nz) * 2 + 1 - y
         arrive(l_all.at[src], ly_sem, (d,))
@@ -141,14 +149,18 @@
         gl_out[:, c * GL_LANES : (c + 1) * GL_LANES] = (total * scale_mine[:, :1]).astype(jnp.bfloat16)
 
     gw_acc[...] = jnp.zeros_like(gw_acc)
-
-    def weight_step(step, carry):
+    piece_chans = chans // gw_r.shape[0]
+
+    def weight_step(piece, step):
         rt = right_t[pl.ds(pl.multiple_of(step * jb, jb), jb), :]
-        for ac in range(0, chans, 2):
+        begin, end = piece * piece_chans, (piece + 1) * piece_chans
+        for ac in range(begin, end, 2):
             at = slice(ac * rows, (ac + 2) * rows)
-            oh[:, at], ol[:, at] = split(dot(rt, left[:, at], NN))
-        for ac in range(0, chans, 8):
-            total = gw_acc[ac * chans : (ac + 8) * chans, :]
+            to = slice((ac - begin) * rows, (ac - begin + 2) * rows)
+            oh[:, to], ol[:, to] = split(dot(rt, left[:, at], NN))
+        for ac in range(0, piece_chans, 8):
+            out = slice((begin + ac) * chans, (begin + ac + 8) * chans)
+            total = gw_acc[out, :]
             for jp in range(step_cols // 2):
                 block = p_ref[pl.ds(step * step_cols + 2 * jp, 2)].reshape(2 * rows, width)
                 for src in (oh, ol):
@@ -166,74 +178,95 @@
                         axis=0,
                     )
                     total += dot(lhs, block, NN)
-            gw_acc[ac * chans : (ac + 8) * chans, :] = total
-        return carry
-
-    lax.fori_loop(0, steps // 2, weight_step, 0)
+            gw_acc[out, :] = total
+
+    def weight_steps(piece, start, stop):
+        def one(step, carry):
+            weight_step(piece, step)
+            return carry
+
+        lax.fori_loop(start, stop, one, 0)
+
+    piece_rows = piece_chans * chans
+    half_rows, quarter, last = gw_r.shape[1], gw_y.shape[1], gw_z.shape[2]
+
+    def span(start, size):
+        return pl.ds(pl.multiple_of(start, 8), size)
+
+    def gw_place(h, r, yy, zz):
+        return h * piece_rows + r * half_rows + yy * quarter + zz * last
+
+    def gw_row(h):
+        src = gw_acc.at[span(gw_place(h, 1 - row, 0, 0), half_rows)]
+        sent.append(send(src, gw_r.at[h], gws_sem, (h, 0), {"row": 1 - row}))
+
+    def gw_ypair(h):
+        arrive(gw_r.at[h], gws_sem, (h, 0))
+        gw_s1[h] = gw_acc[span(gw_place(h, row, 0, 0), half_rows), :] + gw_r[h]
+        sent.append(send(gw_s1.at[h, span((1 - y) * quarter, quarter)], gw_y.at[h], gws_sem, (h, 1), {"seq": ypeer}))
+
+    def gw_zs(h):
+        arrive(gw_y.at[h], gws_sem, (h, 1))
+        gw_s2[h] = gw_s1[h, span(y * quarter, quarter), :] + gw_y[h]
+        for d in range(1, nz):
+            src = gw_s2.at[h, span(zs[d] * last, last)]
+            sent.append(send(src, gw_z.at[h, z], gwz_sem, (h, d), {"seq": zs[d] * 2 + y}))
+
+    def gw_final(h):
+        total = gw_s2[h, span(z * last, last), :]
+        for d in range(1, nz):
+            src = lax.rem(z + nz - d, nz)
+            arrive(gw_z.at[h, src], gwz_sem, (h, d))
+            total += gw_z[h, src]
+        mine = span(gw_place(h, row, y, z), last)
+        gw_f[mine, :] = total / count
+        for d in range(1, nz):
+            sent.append(send(gw_f.at[mine], gw_f.at[mine], gwg_sem, (h, d), {"seq": zs[d] * 2 + y}))
+
+    def gw_gather_y(h):
+        for d in range(1, nz):
+            src = lax.rem(z + nz - d, nz)
+            arrive(gw_f.at[span(gw_place(h, row, y, src), last)], gwg_sem, (h, d))
+        mine = span(gw_place(h, row, y, 0), quarter)
+        sent.append(send(gw_f.at[mine], gw_f.at[mine], gws_sem, (h, 2), {"seq": ypeer}))
+
+    def gw_gather_row(h):
+        arrive(gw_f.at[span(gw_place(h, row, 1 - y, 0), quarter)], gws_sem, (h, 2))
+        mine = span(gw_place(h, row, 0, 0), half_rows)
+        sent.append(send(gw_f.at[mine], gw_f.at[mine], gws_sem, (h, 3), {"row": 1 - row}))
+
+    def gw_done(h):
+        arrive(gw_f.at[span(gw_place(h, 1 - row, 0, 0), half_rows)], gws_sem, (h, 3))
+
+    pieces = range(gw_r.shape[0])
+    last_piece = len(pieces) - 1
+    middle = steps // 2
+    weight_steps(0, 0, middle)
     for c in range(chunks // 2):
         gl_second(c)
-    lax.fori_loop(steps // 2, steps, weight_step, 0)
-
-    half_rows, quarter, last = gw_r.shape[0], gw_y.shape[0], gw_z.shape[1]
-
-    def span(start, size):
-        return pl.ds(pl.multiple_of(start, 8), size)
-
-    def gw_row():
-        sent.append(send(gw_acc.at[span((1 - row) * half_rows, half_rows)], gw_r, gws_sem, (0,), {"row": 1 - row}))
-
-    def gw_ypair():
-        arrive(gw_r, gws_sem, (0,))
-        gw_s1[...] = gw_acc[span(row * half_rows, half_rows), :] + gw_r[...]
-        sent.append(send(gw_s1.at[span((1 - y) * quarter, quarter)], gw_y, gws_sem, (1,), {"seq": ypeer}))
-
-    def gw_zs():
-        arrive(gw_y, gws_sem, (1,))
-        gw_s2[...] = gw_s1[span(y * quarter, quarter), :] + gw_y[...]
-        for d in range(1, nz):
-            sent.append(send(gw_s2.at[span(zs[d] * last, last)], gw_z.at[z], gwz_sem, (d,), {"seq": zs[d] * 2 + y}))
-
-    def gw_place(r, yy, zz):
-        return r * half_rows + yy * quarter + zz * last
-
-    def gw_final():
-        total = gw_s2[span(z * last, last), :]
-        for d in range(1, nz):
-            src = lax.rem(z + nz - d, nz)
-            arrive(gw_z.at[src], gwz_sem, (d,))
-            total += gw_z[src]
-        mine = span(gw_place(row, y, z), last)
-        gw_f[mine, :] = total / count
-        for d in range(1, nz):
-            sent.append(send(gw_f.at[mine], gw_f.at[mine], gwg_sem, (d,), {"seq": zs[d] * 2 + y}))
-
-    def gw_gather_y():
-        for d in range(1, nz):
-            arrive(gw_f.at[span(gw_place(row, y, lax.rem(z + nz - d, nz)), last)], gwg_sem, (d,))
-        mine = span(gw_place(row, y, 0), quarter)
-        sent.append(send(gw_f.at[mine], gw_f.at[mine], gws_sem, (2,), {"seq": ypeer}))
-
-    def gw_gather_row():
-        arrive(gw_f.at[span(gw_place(row, 1 - y, 0), quarter)], gws_sem, (2,))
-        mine = span(gw_place(row, 0, 0), half_rows)
-        sent.append(send(gw_f.at[mine], gw_f.at[mine], gws_sem, (3,), {"row": 1 - row}))
-
-    def gw_done():
-        arrive(gw_f.at[span(gw_place(1 - row, 0, 0), half_rows)], gws_sem, (3,))
-        gw_out[...] = gw_f[...]
-
-    gw_row()
+    weight_steps(0, middle, steps)
+    gw_row(0)
+    if last_piece:
+        weight_steps(1, 0, middle)
+    gw_ypair(0)
     for c in range(chunks // 2, chunks):
         gl_second(c)
-
-    between = {0: gw_ypair, 1: gw_zs, 3: gw_final, 4: gw_gather_y}
+    if last_piece:
+        weight_steps(1, middle, steps)
+        gw_row(1)
+    gw_zs(0)
+
+    between = {2: [lambda: gw_final(0)]}
+    if last_piece:
+        between[0] = [lambda: gw_ypair(1)]
+        between[4] = [lambda: gw_zs(1)]
     for step in range(max(steps, 6)):
         if step < steps:
             at = slice(step * jb, (step + 1) * jb)
             g = dot(qh[at, :], left[...], NT) + dot(ql[at, :], left[...], NT)
             gr_t[:, :, at] = g.T.reshape(shards, seq_rows, jb)
-        if step in between:
-            between[step]()
+        for act in between.get(step, []):
+            act()
 
     collector = lax.div(me, nz) == row
     slot = lax.rem(me, nz)
@@ -255,7 +288,9 @@
     def _():
         row_copy().start()
 
-    gw_gather_row()
+    gw_gather_y(0)
+    if last_piece:
+        gw_final(1)
 
     @pl.when(collector)
     def _():
@@ -266,9 +301,16 @@
             right_copy(o).start()
         gr_in[slot] = gr_b[me]
 
+    gw_gather_row(0)
+    if last_piece:
+        gw_gather_y(1)
     for c in range(chunks):
         gl_last(c)
-    gw_done()
+    if last_piece:
+        gw_gather_row(1)
+    for h in pieces:
+        gw_done(h)
+    gw_out[...] = gw_f[...]
 
     for k in range(nz):
         @pl.when(row * nz + k != me)
@@ -300,7 +342,8 @@
     jb = block_cols(cols) * chans
     chunks = lanes // GL_LANES
     total = chans * chans
-    half, quarter, last = total // 2, total // 4, total // 4 // nz
+    pieces = HALVES if total // HALVES // 4 // nz >= 8 else 1
+    half, quarter, last = total // pieces // 2, total // pieces // 4, total // pieces // 4 // nz
     f32, bf16 = jnp.float32, jnp.bfloat16
     flops = 2 * cols * rows * chans * chans * (width * 3 + seqs * 5)
     vmem = pl.BlockSpec(memory_space=pltpu.VMEM)
@@ -317,8 +360,8 @@
         scratch_shapes=[
             pltpu.VMEM((own, lanes), bf16),
             pltpu.VMEM((own, lanes), bf16),
-            pltpu.VMEM((jb, lanes), bf16),
-            pltpu.VMEM((jb, lanes), bf16),
+            pltpu.VMEM((jb, lanes // pieces), bf16),
+            pltpu.VMEM((jb, lanes // pieces), bf16),
             pltpu.VMEM((shards, seq_rows, lanes), bf16),
             pltpu.VMEM((shards, seq_rows, LANE + own), bf16),
             pltpu.VMEM((seqs, lanes), bf16),
@@ -333,11 +376,11 @@
             pltpu.VMEM((shards, seq_rows, own), bf16),
             pltpu.VMEM((nz, seq_rows, own), bf16),
             pltpu.VMEM((total, width), f32),
-            pltpu.VMEM((half, width), f32),
-            pltpu.VMEM((half, width), f32),
-            pltpu.VMEM((quarter, width), f32),
-            pltpu.VMEM((quarter, width), f32),
-            pltpu.VMEM((nz, last, width), f32),
+            pltpu.VMEM((pieces, half, width), f32),
+            pltpu.VMEM((pieces, half, width), f32),
+            pltpu.VMEM((pieces, quarter, width), f32),
+            pltpu.VMEM((pieces, quarter, width), f32),
+            pltpu.VMEM((pieces, nz, last, width), f32),
             pltpu.VMEM((total, width), f32),
             sem((2, shards)),
             sem((2, nz)),
@@ -346,9 +389,9 @@
             sem((2, chunks, nz)),
             sem((2,)),
             sem((2, shards)),
-            sem((2, 4)),
-            sem((2, nz)),
-            sem((2, nz)),
+            sem((2, pieces, 4)),
+            sem((2, pieces, nz)),
+            sem((2, pieces, nz)),
         ],
         compiler_params=pltpu.CompilerParams(
             vmem_limit_bytes=56 * 2**20, collective_id=0, has_side_effects=True

time: 75.5 us -> 73 us (0.967)
  Pallas kernels: 63.4 us -> 60.9 us
    pallas_call x1, Pallas kernels: 63.4 us -> 60.9 us  [all_grads(): pl.pallas_call(functools.partial(kernel, shards, chans), in_specs=[vmem]...]
where the time goes in v1:
time: 73 us; the launch traced here: 72.8 us
  Pallas kernels  60.9 us (83%)
  local copies, waits for them, and re-layouts  7.81 us (11%)
  other arithmetic  3.41 us (5%)
    pallas_call x1, Pallas kernels, all_grads(): pl.pallas_call(functools.partial(kernel, shards, chans), in_specs=[vmem]...  60.9 us
    unnamed x8, local copies, waits for them, and re-layouts  3.89 us
    reshape x1, local copies, waits for them, and re-layouts, body(): grad_left = gl.reshape(seq_rows, chans, pair_rows).transpose(0, 2, 1)  1.54 us

profile of v1, /device:TPU:1, one launch (start us, length us, event | category | flops | bytes accessed | tf_op | source)
XLA Modules:
  0.0 72.8 jit_solution(4981176754590889645)
XLA Ops:
  0.6 0.7 convert_element_type.3
  1.3 0.1 broadcast_in_dim.2
  1.4 0.9 %multiply_bitcast_fusion = bf16[1,8,32,128]{3,2,1,0:T(8,128)(2,1)S(1)} fusion(bf16[8,128,32]{1,2,0:T(8,128)(2,1)} %param.5, bf16[8]{0:T(256)(128)(2,1)S(1)} %convert_element_type.3), kind=kLoop, calls=%fused_computation.5 | loop fusion | flops 32768 | bytes 131088
  2.3 0.7 copy.21
  2.9 0.0 copy-start
  2.9 1.1 %broadcast_multiply_fusion = bf16[8,384,32]{1,2,0:T(8,128)(2,1)S(1)} fusion(bf16[8,384,32]{1,2,0:T(8,128)(2,1)} %param.6, bf16[8]{0:T(256)(128)(2,1)S(1)} %convert_element_type.3), kind=kLoop, calls=%fused_computation.2 | loop fusion | flops 98304 | bytes 393232 | tf_op jit(solution)/shard_map/mul | solution.py:410
  4.1 0.4 copy.11
  4.5 0.7 %reshape.20 = bf16[8,8,1536]{2,1,0:T(8,128)(2,1)S(1)} reshape(bf16[8,384,32]{2,1,0:T(8,128)(2,1)S(1)} %copy.11) | data formatting | bytes 393216 | tf_op jit(solution)/shard_map/reshape | solution.py:410
  5.2 0.1 copy.12
  5.3 0.7 maximum_bitcast_fusion.r_in
  6.0 0.0 copy-done
  6.0 1.6 %copy.20 = bf16[128,48,128]{2,0,1:T(8,128)(2,1)} copy(bf16[128,48,128]{2,1,0:T(8,128)(2,1)S(1)} %copy-done) | data formatting | bytes 3145728 | tf_op args[2]
  7.5 60.9 %all_grads.1 = (bf16[8,4096]{1,0:T(8,128)(2,1)}, bf16[4,8,1536]{2,1,0:T(8,128)(2,1)}, f32[1024,128]{1,0:T(8,128)}) custom-call(bf16[48,128,128]{2,1,0:T(8,128)(2,1)} %bitcast.16, bf16[1024,128]{1,0:T(8,128)(2,1)} %w_ref.1, bf16[8,4096]{1,0:T(8,128)(2,1)} %bitcast.18, bf16[8,8,1664]{2,1,0:T(8,128)(2,1)} %maximum_bitcast_fusion.r_in), custom_call_target="tpu_custom_call" | custom-call | flops 8858370048 | bytes 6291456 | tf_op jit(solution)/shard_map/all_grads/pallas_call | solution.py:351
  68.4 0.0 copy-start.1
  68.4 1.5 %copy.22 = bf16[8,32,128]{2,1,0:T(8,128)(2,1)} copy(bf16[8,32,128]{2,0,1:T(8,128)(2,1)} %bitcast.20) | data formatting | bytes 131072 | tf_op jit(solution)/shard_map/reshape | solution.py:414
  70.0 0.9 %copy.14 = bf16[8,4,1536]{2,1,0:T(4,128)(2,1)S(1)} copy(bf16[8,4,1536]{2,0,1:T(8,128)(2,1)} %bitcast.17) | data formatting | bytes 196608 | tf_op jit(solution)/shard_map/transpose | solution.py:415
  70.9 0.2 reshape.22
  71.1 0.8 %copy.15 = bf16[8,192,32]{1,2,0:T(8,128)(2,1)} copy(bf16[8,192,32]{2,1,0:T(8,128)(2,1)S(1)} %reshape.22) | data formatting | bytes 196608
  72.0 0.0 copy-done.1
  72.0 0.8 %copy.24 = f32[1024,128]{1,0:T(8,128)} copy(f32[1024,128]{1,0:T(8,128)S(1)} %copy-done.1) | data formatting | bytes 1048576
Async XLA Ops:
  2.9 3.0 %copy-start = (bf16[128,48,128]{2,1,0:T(8,128)(2,1)S(1)}, bf16[128,48,128]{2,1,0:T(8,128)(2,1)}, u32[]{:S(2)}) copy-start(bf16[128,48,128]{2,1,0:T(8,128)(2,1)} %param.7) | copy-start | bytes 4718596
  68.4 3.6 %copy-start.1 = (f32[1024,128]{1,0:T(8,128)S(1)}, f32[1024,128]{1,0:T(8,128)}, u32[]{:S(2)}) copy-start(f32[1024,128]{1,0:T(8,128)} %get-tuple-element.17) | copy-start | bytes 1572868
